TPU v7x, 32 devices: a whole 2x2x4 slice. The times are simulated.
32 devices in a mesh: outer: 4 (over z), inner: 8 (over y, x, core).
Axes of the slice: x: 2, y: 2, z: 4, core: 2. Of those that a mesh axis runs over, the one named last changes fastest.
Arguments:
- normals: bfloat16 [512, 128, 512], P('outer', 'inner'), may hold values from -6 to 6
- states: bfloat16 [512, 512], P('outer'), may hold values from -0.29882812 to 0.29882812
- loadings: bfloat16 [2048, 512], replicated, may hold values from -6 to 6
- strikes: float32 [2048], replicated, may hold values from -6 to 6
- hedge: float32 [2048], replicated, may hold values from -384 to 384
- sigma: float32 [512], replicated, may hold values from 0.02 to 0.1
- tail: int32 [128], replicated, may hold values from 0 to 511, as said below
Outputs:
- grad: float32 [2048, 512], P(('outer', 'inner'))
Inputs may be any that keep to these rules, and one draw needn't show every extreme that they name: Increasing and distinct. Group g holds nodes g * 128 to (g + 1) * 128 - 1; at most 80 tail indices fall into one group, and some group holds exactly 80.
All inputs are finite; a program needn't handle non-finite values.
Results may differ from a plain program's by a relative error of at most 0.00057.
Values may be sent and summed in bfloat16 or wider, within the bound.
No kernel may reach another device: no remote copies, remote signals or barrier semaphores. Data moves between devices by JAX's collectives and lax.ppermute only.
A program may use at most 64 MiB of HBM per device.

v0:
```python
import functools

import jax
import jax.numpy as jnp
from jax import lax
from jax.experimental import pallas as pl
from jax.experimental.pallas import tpu as pltpu
from jax.sharding import PartitionSpec as P

CAP = 80
EPSILON = 1e-06
VMEM = pl.BlockSpec(memory_space=pltpu.VMEM)
SMEM = pl.BlockSpec(memory_space=pltpu.SMEM)
HBM = pl.BlockSpec(memory_space=pltpu.HBM)
F32 = jnp.float32
BF16 = jnp.bfloat16
F16 = jnp.float16


def split_of(count, most):
    for size in range(min(count, most), 0, -1):
        if count % size == 0:
            return size
    return 1


def small(mebibytes):
    return pltpu.CompilerParams(vmem_limit_bytes=mebibytes << 20)


def first_of(tail, base):
    count = tail.shape[0]
    first = jnp.int32(0)
    for bit in range(count.bit_length() - 1, -1, -1):
        ahead = first + (1 << bit)
        below = tail[jnp.minimum(ahead, count) - 1] < base
        first = jnp.where((ahead <= count) & below, ahead, first)
    return first


def place_of(tail, first, base, slot):
    at = slot + lax.rem(lax.axis_index("inner"), 2) * (CAP // 2)
    at = first + jnp.where(at >= CAP, at - CAP, at)
    node = tail[jnp.minimum(at, tail.shape[0] - 1)] - base
    return node, at < tail.shape[0]


def gather_kernel(
    part, tail_hbm, normals, chosen_hbm, mine, other,
    tail, chosen, tail_sem, sems, out_sem,
):
    node_count = normals.shape[0]
    tail_copy = pltpu.make_async_copy(tail_hbm, tail, tail_sem)
    tail_copy.start()
    base = lax.axis_index("outer") * node_count
    tail_copy.wait()
    first = first_of(tail, base)
    parts = CAP // part

    @pl.loop(0, parts)
    def _(p):
        for k in range(part):
            slot = p * part + k
            node, inside = place_of(tail, first, base, slot)
            used = inside & (node >= 0) & (node < node_count)
            node = jnp.where(used, node, lax.rem(slot, node_count))
            pltpu.make_async_copy(normals.at[node], chosen.at[slot], sems.at[p]).start()

    out_copy = pltpu.make_async_copy(chosen, chosen_hbm, out_sem)
    for begin, sums in ((0, mine), (parts // 2, other)):

        @pl.loop(0, parts // 2)
        def _(p):
            piece = chosen.at[pl.ds((begin + p) * part, part)]
            pltpu.make_async_copy(piece, piece, sems.at[begin + p]).wait()
            there = chosen_hbm.at[pl.ds((begin + p) * part, part)]
            pltpu.make_async_copy(piece, there, out_sem).start()
            values = piece[...].astype(F32)
            rows = pl.ds(pl.multiple_of(p * part, part), part)
            sums[0, rows, :] = jnp.sum(values, axis=1)
            sums[1, rows, :] = jnp.sum(values * values, axis=1)

    out_copy.wait()


def gather_nodes(tail, normals):
    _, paths, factors_n = normals.shape
    part = split_of(CAP // 2, 8)
    sums = jax.ShapeDtypeStruct((2, CAP // 2, factors_n), F32)
    chosen = (CAP, paths, factors_n)
    return pl.pallas_call(
        functools.partial(gather_kernel, part),
        in_specs=[HBM, HBM],
        out_specs=[HBM, VMEM, VMEM],
        out_shape=[
            pltpu.HBM(chosen, BF16),
            sums,
            sums,
        ],
        scratch_shapes=[
            pltpu.SMEM(tail.shape, jnp.int32),
            pltpu.VMEM(chosen, BF16),
            pltpu.SemaphoreType.DMA,
            pltpu.SemaphoreType.DMA((CAP // part,)),
            pltpu.SemaphoreType.DMA,
        ],
        compiler_params=small(8),
        cost_estimate=pl.CostEstimate(flops=0, bytes_accessed=0, transcendentals=0),
        name="gather_nodes",
    )(tail, normals)


def to_message(sums, within):
    high = sums.astype(F16)
    low = (sums - high.astype(F32)).astype(F16)
    return jnp.stack([high, low, within.astype(F16)])


def pooled(parts, count):
    total = sum(s for s, _ in parts)
    center = total / (count * len(parts))
    return total, sum(w + (s / count - center) ** 2 * count for s, w in parts)


def of_message(message):
    high, low, within = message.astype(F32)
    return high + low, within


def order_kernel(
    unit, bound, plan, far, tail_hbm, states_hbm, loadings_hbm, strikes, hedge,
    levels, live, gain, *refs,
):
    chunks, rows = len(plan), gain.shape[0]
    cells = [(chunk, step) for chunk in range(chunks) for step in range(len(plan[chunk]))]
    ordered, terms = refs[:chunks], refs[chunks : 2 * chunks]
    tail, states, onehot, own, tail_sem, states_sem, sems = refs[2 * chunks :]
    node_count = states.shape[0]
    position = lax.axis_index("inner")
    group, chip, core = lax.axis_index("outer"), position // 2, lax.rem(position, 2)
    tail_copy = pltpu.make_async_copy(tail_hbm, tail, tail_sem)
    states_copy = pltpu.make_async_copy(states_hbm, states, states_sem)
    tail_copy.start()
    states_copy.start()
    blocks, copies = [], []
    for k, (chunk, step) in enumerate(cells):
        d, away = plan[chunk][step]
        to_chip, to_group = far(chip, d, group, away)
        block = (to_group * (lax.axis_size("inner") // 2) + to_chip) * 2 + core
        copy = pltpu.make_async_copy(loadings_hbm.at[block], own.at[k], sems.at[k])
        copy.start()
        blocks.append(block)
        copies.append(copy)
    wide = strikes.shape[1]
    lanes = lax.broadcasted_iota(jnp.int32, (rows, wide), 1)
    lines = lax.broadcasted_iota(jnp.int32, (rows, wide), 0)

    def column(ref, block):
        line = ref[pl.ds(block * rows // wide, 1), :]
        here = lanes == lines + lax.rem(block * rows, wide)
        return jnp.sum(jnp.where(here, line, 0.0), axis=1, keepdims=True)

    for k, block in enumerate(blocks):
        chunk, step = cells[k]
        at = slice(step * rows, (step + 1) * rows)
        size = column(hedge, block)
        scale = jnp.abs(size)
        terms[chunk][at, 0:1] = column(strikes, block) * 0.5
        terms[chunk][at, 1:2] = size * 0.5
        terms[chunk][at, 2:3] = jnp.where(
            scale > 1e-30, bound / jnp.maximum(scale, 1e-30), 0.0
        )
        if plan[chunk][step] == (0, 0):
            owned = scale * unit
    tail_copy.wait()
    base = group * node_count
    first = first_of(tail, base)
    nodes = lax.broadcasted_iota(jnp.int32, (1, node_count), 1)
    for slot in range(CAP):
        node, inside = place_of(tail, first, base, slot)
        used = inside & (node >= 0) & (node < node_count)
        onehot[slot : slot + 1, :] = ((nodes == node) & used).astype(F32)
        if slot < CAP // 2:
            live[slot : slot + 1, :] = jnp.full((1, live.shape[1]), used.astype(F32))
    states_copy.wait()
    levels[...] = jnp.dot(
        onehot[...].astype(BF16), states[...], preferred_element_type=F32
    )
    for k, copy in enumerate(copies):
        copy.wait()
        values = own[k].astype(F32)
        chunk, step = cells[k]
        if plan[chunk][step] == (0, 0):
            gain[...] = values * owned
        ordered[chunk][step] = (values * 0.5).astype(BF16)


def order(unit, bound, plan, far, tail, states, loadings, strikes, hedge):
    chunks, cells = len(plan), sum(len(part) for part in plan)
    _, rows, factors_n = loadings.shape
    return pl.pallas_call(
        functools.partial(order_kernel, unit, bound, plan, far),
        in_specs=[HBM] * 3 + [VMEM] * 2,
        out_specs=[VMEM] * (2 * chunks + 3),
        out_shape=[
            jax.ShapeDtypeStruct((count, factors_n), F32) for count in (CAP, CAP // 2, rows)
        ]
        + [jax.ShapeDtypeStruct((len(part), rows, factors_n), BF16) for part in plan]
        + [jax.ShapeDtypeStruct((len(part) * rows, 3), F32) for part in plan],
        scratch_shapes=[
            pltpu.SMEM(tail.shape, jnp.int32),
            pltpu.VMEM(states.shape, BF16),
            pltpu.VMEM((CAP, states.shape[0]), F32),
            pltpu.VMEM((cells, rows, factors_n), BF16),
            pltpu.SemaphoreType.DMA,
            pltpu.SemaphoreType.DMA,
            pltpu.SemaphoreType.DMA((cells,)),
        ],
        compiler_params=small(12),
        cost_estimate=pl.CostEstimate(flops=0, bytes_accessed=1 << 20, transcendentals=0),
        name="order_instruments",
    )(tail, states, loadings, strikes, hedge)


def prepare(own, theirs, stats, levels, sigma, scaled, factors, ready, begin, end):
    slots, paths, factors_n = own.shape
    half = slots // 2
    shape = (paths, factors_n)
    sigmas = jnp.broadcast_to(sigma[...], shape)
    for at in range(begin, end):
        mine, row = at < half, at % half
        slot = row if mine == ready else row + half
        source = own if mine else theirs
        place = slot if mine else (slot + half) % slots
        center = jnp.broadcast_to(stats[0, row : row + 1, :], shape)
        rstd = jnp.broadcast_to(stats[1, row : row + 1, :], shape)
        level = jnp.broadcast_to(levels[place : place + 1, :], shape)
        unit = ((source[slot].astype(F32) - center) * rstd).astype(BF16)
        rows = slice(at * paths, (at + 1) * paths)
        scaled[rows, :] = unit
        factors[rows, :] = (level + sigmas * unit.astype(F32)).astype(BF16)


def ready_kernel(own, theirs, stats, levels, sigma, loadings, terms, scaled, factors, out):
    slots, paths, _ = own.shape
    prepare(own, theirs, stats, levels, sigma, scaled, factors, True, 0, slots)
    out[...] = cross_of(slots * paths, ((scaled, factors),), loadings, terms)


def ready_rows(own, theirs, stats, levels, sigma, ordered, terms):
    slots, paths, factors_n = own.shape
    rows = slots * paths
    count = ordered.shape[0]
    half = jax.ShapeDtypeStruct((rows, factors_n), BF16)
    return pl.pallas_call(
        ready_kernel,
        in_specs=[VMEM] * 7,
        out_specs=[VMEM] * 3,
        out_shape=[half, half, jax.ShapeDtypeStruct((count, factors_n), F32)],
        compiler_params=small(16),
        cost_estimate=cost_of(rows, count, factors_n),
        name="ready_rows",
    )(own, theirs, stats, levels, sigma, ordered, terms)


def cross_of(tile, halves, loadings, terms):
    strikes, hedge, scale = terms[:, 0:1], terms[:, 1:2], terms[:, 2:3]
    part = loadings[...]
    each = halves[0][0].shape[0] // tile
    places = [(half, r * tile) for half in range(len(halves)) for r in range(each)]

    def level(half, at):
        rows = halves[half][1][at : at + tile, :]
        return lax.dot_general(
            part, rows, (((1,), (1,)), ((), ())), preferred_element_type=F32
        )

    total = None
    current = level(*places[0])
    for k, (half, at) in enumerate(places):
        after = level(*places[k + 1]) if k + 1 < len(places) else None
        weight = (jnp.tanh(current - strikes) * hedge + hedge).astype(BF16)
        cross = jnp.dot(
            weight, halves[half][0][at : at + tile, :], preferred_element_type=F32
        )
        total = cross if total is None else total + cross
        current = after
    return total * scale


def first_kernel(
    own, theirs, stats, levels, sigma, done, loadings, terms, scaled, factors, *outs
):
    slots, paths, _ = own.shape
    prepare(own, theirs, stats, levels, sigma, scaled, factors, False, 0, slots)
    sums = cross_of(slots * paths, ((scaled, factors),), loadings, terms)
    give(done[...] + sums, *outs)


def next_kernel(tile, s0, f0, s1, f1, loadings, terms, *outs):
    give(cross_of(tile, ((s0, f0), (s1, f1)), loadings, terms), *outs)


def give(sums, *outs):
    at = 0
    for out in outs:
        out[...] = sums[at : at + out.shape[0]]
        at += out.shape[0]


def cost_of(rows, count, factors_n):
    return pl.CostEstimate(
        flops=2 * rows * count * factors_n,
        bytes_accessed=4 * count * factors_n,
        transcendentals=0,
    )


def tile_of(slots, paths):
    return paths * split_of(slots, max(1, 1280 // paths))


def first_chunk(sizes, own, theirs, stats, levels, sigma, done, ordered, terms):
    slots, paths, factors_n = own.shape
    count = ordered.shape[0]
    half = jax.ShapeDtypeStruct((slots * paths, factors_n), BF16)
    return pl.pallas_call(
        first_kernel,
        in_specs=[VMEM] * 8,
        out_specs=[VMEM] * (2 + len(sizes)),
        out_shape=[half, half] + [jax.ShapeDtypeStruct((n, factors_n), F32) for n in sizes],
        compiler_params=small(16),
        cost_estimate=cost_of(slots * paths, count, factors_n),
        name="first_chunk",
    )(own, theirs, stats, levels, sigma, done, ordered, terms)


def next_chunk(sizes, tile, ready, rest, ordered, terms):
    rows, factors_n = ready[0].shape
    count = ordered.shape[0]
    return pl.pallas_call(
        functools.partial(next_kernel, tile),
        in_specs=[VMEM] * 6,
        out_specs=[VMEM] * len(sizes),
        out_shape=[jax.ShapeDtypeStruct((n, factors_n), F32) for n in sizes],
        compiler_params=small(16),
        cost_estimate=cost_of(2 * rows, count, factors_n),
        name="next_chunk",
    )(*ready, *rest, ordered, terms)


def body(normals, states, loadings, strikes, hedge, sigma, tail):
    groups = lax.axis_size("outer")
    inner = lax.axis_size("inner")
    chips = inner // 2
    _, per_node, factors_n = normals.shape
    instruments = loadings.shape[0]
    tail_count = tail.shape[0]
    paths = per_node * inner
    rows = instruments // (groups * inner)
    paired = chips & (chips - 1) == 0

    def partner(of, d):
        return of ^ d if paired else (of + d) % chips

    def beyond(of, s):
        return of ^ s if groups & (groups - 1) == 0 else (of + s) % groups

    def to_core(x):
        return lax.ppermute(x, "inner", [(i, i ^ 1) for i in range(inner)])

    def to_chip(x, d):
        return lax.ppermute(
            x, "inner", [(i, partner(i // 2, d) * 2 + i % 2) for i in range(inner)]
        )

    def to_group(x, s):
        return lax.ppermute(x, "outer", [(g, beyond(g, s)) for g in range(groups)])

    bound = 32768.0 / (tail_count * paths)
    unit = 1.0 / (bound * tail_count * paths)

    tail, normals, states, loadings = (
        pltpu.with_memory_space_constraint(x, pltpu.HBM)
        for x in (tail, normals, states, loadings.reshape(groups * inner, rows, factors_n))
    )
    wide = 128 if 128 % rows == 0 else rows
    strikes, hedge = strikes.reshape(-1, wide), hedge.reshape(-1, wide)

    chosen, mine, other = gather_nodes(tail, normals)
    sums, squares = mine + to_core(other)
    count = 2 * per_node
    within = squares - sums * sums / count
    message = to_message(sums, within)
    chosen, message, strikes = lax.optimization_barrier((chosen, message, strikes))
    rounds = [1 << k for k in range(chips.bit_length() - 1)] if paired and chips > 4 else []
    if not rounds:
        arrived = [of_message(to_chip(message, d)) for d in range(chips - 1, 0, -1)]
        sums, within = pooled([(sums, within), *arrived], count)
        count *= chips
    for d in rounds:
        arrived = to_chip(message, d)
        sums, within = pooled([(sums, within), of_message(arrived)], count)
        count *= 2
        if d != rounds[-1]:
            message = to_message(sums, within)
    theirs = to_core(chosen)
    steps = range(groups)
    relayed = chips == 4 and groups % 2 == 0
    if relayed:
        half = groups // 2
        low, high = steps[:half], steps[half:]
        plan = [
            [(3, s) for s in steps],
            [(1, s) for s in high] + [(2, s) for s in high] + [(0, s) for s in steps],
            [(2, s) for s in low] + [(1, s) for s in low],
        ]
        first_sizes = (half * rows,) * 2
    else:
        plan = [[(d, s) for s in steps] for d in range(chips - 1, -1, -1)]
        first_sizes = (groups * rows,)
    far = lambda chip, d, group, s: (partner(chip, d), beyond(group, s))
    levels, live, gain, *parts = order(
        unit, bound, plan, far, tail, states, loadings, strikes, hedge
    )
    ordered = [part.reshape(-1, factors_n) for part in parts[: len(plan)]]
    terms = parts[len(plan) :]
    sums, within, theirs, levels, live, gain, ordered, terms = lax.optimization_barrier(
        (sums, within, theirs, levels, live, gain, ordered, terms)
    )
    stats = jnp.stack([sums / count, live * lax.rsqrt(within / count + EPSILON)])
    their_stats = to_core(stats)

    sigmas = sigma.reshape(1, factors_n)
    *ready, done = ready_rows(chosen, theirs, stats, levels, sigmas, ordered[0], terms[0])

    tile = tile_of(CAP, per_node)
    results = first_chunk(
        first_sizes, chosen, theirs, their_stats, levels, sigmas, done, ordered[0], terms[0]
    )
    rest, first = tuple(results[:2]), results[2:]

    def chunk(k, sizes, *after):
        kept, _ = lax.optimization_barrier((rest, after))
        return next_chunk(sizes, tile, ready, kept, ordered[k], terms[k])

    def plus(x, y):
        return x + y.astype(F32)

    if relayed:
        size = half * rows
        a3, b3 = (x.astype(F16) for x in first)
        from_b3, from_a3 = to_chip(b3, 1), to_chip(a3, 2)
        b1, b2, a0, b0 = chunk(1, (size,) * 4, a3, b3)
        b1, b2 = b1.astype(F16), plus(b2, from_b3).astype(F16)
        from_b1, from_b2 = to_chip(b1, 1), to_chip(b2, 2)
        a2, a1 = chunk(2, (size,) * 2, b1, b2)
        a2, a1 = a2.astype(F16), plus(a1, from_a3).astype(F16)
        from_a2, from_a1 = to_chip(a2, 2), to_chip(a1, 1)
        b0, _ = lax.optimization_barrier((b0, (a2, a1)))
        kept_b = plus(plus(b0, from_b1), from_b2)
        sent = [kept_b[k * rows :][:rows].astype(F16) for k in range(half)]
        sent, a0 = lax.optimization_barrier((sent, a0))
        kept_a = plus(plus(a0, from_a2), from_a1)
        sent = [kept_a[k * rows :][:rows].astype(F16) for k in range(1, half)] + sent
        owned = kept_a[:rows]
    else:
        arrived = []
        (kept,) = first
        for k in range(1, chips):
            sent = kept.astype(F16)
            arrived.append(to_chip(sent, chips - k))
            (kept,) = chunk(k, first_sizes, sent)
        for item in arrived:
            kept = plus(kept, item)
        sent = [kept[s * rows :][:rows].astype(F16) for s in range(1, groups)]
        owned = kept[:rows]
    far_sums = None
    for s in range(max(1, groups // 2), groups):
        item = to_group(sent[s - 1], s).astype(F32)
        far_sums = item if far_sums is None else far_sums + item
    far_sums = lax.optimization_barrier(far_sums)
    for s in range(1, max(1, groups // 2)):
        owned = plus(owned, to_group(sent[s - 1], s))
    owned = owned + far_sums
    return gain * owned


def solution(mesh):
    placed = (P("outer", "inner", None), P("outer", None), P(), P(), P(), P(), P())
    return jax.shard_map(
        body, mesh=mesh, in_specs=placed, out_specs=P(("outer", "inner"), None), check_vma=False
    )
```

profile of v0, /device:TPU:0, one launch (start us, length us, event | category | flops | bytes accessed | tf_op | source)
XLA Modules:
  0.0 41.1 jit_solution(16833658281609138629)
XLA Ops:
  0.0 0.0 copy-start.2
  0.0 0.0 copy-start.3
  0.0 3.3 %gather_nodes.1 = (bf16[80,16,512]{2,1,0:T(8,128)(2,1)}, f32[2,40,512]{2,1,0:T(8,128)S(1)}, f32[2,40,512]{2,1,0:T(8,128)S(1)}) custom-call(s32[128]{0:T(128)} %tail_hbm.3, bf16[128,16,512]{2,1,0:T(8,128)(2,1)} %normals.1), custom_call_target="tpu_custom_call" | custom-call | tf_op jit(solution)/shard_map/gather_nodes/pallas_call | solution.py:91
  3.3 0.5 %collective-permute-start = (f32[2,40,512]{2,1,0:T(8,128)S(1)}, f32[2,40,512]{2,1,0:T(8,128)S(1)}, u32[]{:S(2)}, u32[]{:S(2)}) collective-permute-start(f32[2,40,512]{2,1,0:T(8,128)S(1)} %get-tuple-element.54), channel_id=1, source_target_pairs={{0,1},{1,0},{2,3},{3,2},{4,5},{5,4},{6,7},{7,6},{8,9},{9,8},{10,11... | collective-permute-start | bytes 491528 | tf_op jit(solution)/shard_map/ppermute | solution.py:370
  3.8 1.0 %collective-permute-done = f32[2,40,512]{2,1,0:T(8,128)S(1)} collective-permute-done((f32[2,40,512]{2,1,0:T(8,128)S(1)}, f32[2,40,512]{2,1,0:T(8,128)S(1)}, u32[]{:S(2)}, u32[]{:S(2)}) %collective-permute-start) | collective-permute-done | bytes 163872 | tf_op jit(solution)/shard_map/ppermute | solution.py:370
  5.0 0.4 %collective-permute-start.4 = (bf16[80,16,512]{2,1,0:T(8,128)(2,1)}, bf16[80,16,512]{2,1,0:T(8,128)(2,1)S(1)}, u32[]{:S(2)}, u32[]{:S(2)}) collective-permute-start(bf16[80,16,512]{2,1,0:T(8,128)(2,1)} %get-tuple-element.57.own), channel_id=1, source_target_pairs={{0,1},{1,0},{2,3},{3,2},{4,5},{5,4},{6,7},{7,6},{8,9},{9,8},{10,11... | collective-permute-start | bytes 3932168 | tf_op jit(solution)/shard_map/ppermute | solution.py:370
  5.4 2.6 %collective-permute-start.3 = (f16[3,40,512]{2,1,0:T(8,128)(2,1)S(1)}, f16[3,40,512]{2,1,0:T(8,128)(2,1)S(1)}, u32[]{:S(2)}, u32[]{:S(2)}) collective-permute-start(f16[3,40,512]{2,1,0:T(8,128)(2,1)S(1)} %pad_maximum_fusion.1), channel_id=1, source_target_pairs={{0,2},{1,3},{2,0},{3,1},{4,6},{5,7},{6,4},{7,5},{8,10},{9,11},{10,... | collective-permute-start | bytes 368648 | tf_op jit(solution)/shard_map/ppermute | solution.py:373
  8.1 1.5 %collective-permute-start.2 = (f16[3,40,512]{2,1,0:T(8,128)(2,1)S(1)}, f16[3,40,512]{2,1,0:T(8,128)(2,1)S(1)}, u32[]{:S(2)}, u32[]{:S(2)}) collective-permute-start(f16[3,40,512]{2,1,0:T(8,128)(2,1)S(1)} %pad_maximum_fusion.1), channel_id=1, source_target_pairs={{0,4},{1,5},{2,6},{3,7},{4,0},{5,1},{6,2},{7,3},{8,12},{9,13},{10,... | collective-permute-start | bytes 368648 | tf_op jit(solution)/shard_map/ppermute | solution.py:373
  9.6 0.0 collective-permute-start.1
  9.6 0.0 copy-done.2
  9.6 0.0 copy-done.3
  9.6 2.1 %order_instruments.1 = (f32[80,512]{1,0:T(8,128)S(1)}, f32[40,512]{1,0:T(8,128)S(1)}, f32[64,512]{1,0:T(8,128)S(1)}, bf16[4,64,512]{2,1,0:T(8,128)(2,1)S(1)}, bf...) custom-call(s32[128]{0:T(128)} %tail_hbm.3, ...), custom_call_target="tpu_custom_call" | custom-call | bytes 1048576 | tf_op jit(solution)/shard_map/order_instruments/pallas_call | solution.py:201
  11.7 0.2 collective-permute-done.3
  11.9 0.0 copy-start
  11.9 0.0 copy-start.1
  11.9 4.0 %collective-permute-done.2 = f16[3,40,512]{2,1,0:T(8,128)(2,1)S(1)} collective-permute-done((f16[3,40,512]{2,1,0:T(8,128)(2,1)S(1)}, f16[3,40,512]{2,1,0:T(8,128)(2,1)S(1)}, u32[]{:S(2)}, u32[]{:S(2)}) %collective-permute-start.2) | collective-permute-done | bytes 122912 | tf_op jit(solution)/shard_map/ppermute | solution.py:373
  16.0 0.0 collective-permute-done.1
  16.1 0.1 fusion.3
  16.2 0.0 collective-permute-done.4.theirs
  16.2 0.1 collective-permute-start.5
  16.3 0.0 copy-done
  16.3 0.0 copy-done.1
  16.3 1.4 %ready_rows.1 = (bf16[1280,512]{1,0:T(8,128)(2,1)S(1)}, bf16[1280,512]{1,0:T(8,128)(2,1)S(1)}, f32[256,512]{1,0:T(8,128)S(1)}) custom-call(bf16[80,16,512]{2,1,0:T(8,128)(2,1)S(1)} %copy-done, bf16[80,16,512]{2,1,0:T(8,128)(2,1)S(1)} %collective-permute-done.4.theirs, f32[2,40,512]{2,1,0:T(8,128)S(1)} %pad_maximum_fusion.stats, ...), custom_call_target="tpu_custom_call" | custom-call | flops 335544320 | bytes 524288 | tf_op jit(solution)/shard_map/ready_rows/pallas_call | solution.py:255
  17.7 0.0 collective-permute-done.5.stats
  17.7 1.4 %first_chunk.1 = (bf16[1280,512]{1,0:T(8,128)(2,1)S(1)}, bf16[1280,512]{1,0:T(8,128)(2,1)S(1)}, f32[128,512]{1,0:T(8,128)S(1)}, f32[128,512]{1,0:T(8,128)S(1)}) custom-call(bf16[80,16,512]{2,1,0:T(8,128)(2,1)S(1)} %copy-done, bf16[80,16,512]{2,1,0:T(8,128)(2,1)S(1)} %collective-permute-done.4.theirs, f32[2,40,512]{2,1,0:T(8,128)S(1)} %collective-permute-done.5.stats, ...), custom_call_target="tpu_custom_call" | custom-call | flops 335544320 | bytes 524288 | tf_op jit(solution)/shard_map/first_chunk/pallas_call | solution.py:327
  19.2 1.3 %collective-permute-start.6 = (f16[128,512]{1,0:T(8,128)(2,1)S(1)}, f16[128,512]{1,0:T(8,128)(2,1)S(1)}, u32[]{:S(2)}, u32[]{:S(2)}) collective-permute-start(f16[128,512]{1,0:T(8,128)(2,1)S(1)} %convert_element_type.82), channel_id=1, source_target_pairs={{0,2},{1,3},{2,0},{3,1},{4,6},{5,7},{6,4},{7,5},{8,10},{9,11},{10,... | collective-permute-start | bytes 393224 | tf_op jit(solution)/shard_map/ppermute | solution.py:373
  20.5 0.9 %collective-permute-start.7 = (f16[128,512]{1,0:T(8,128)(2,1)S(1)}, f16[128,512]{1,0:T(8,128)(2,1)S(1)}, u32[]{:S(2)}, u32[]{:S(2)}) collective-permute-start(f16[128,512]{1,0:T(8,128)(2,1)S(1)} %convert_element_type.81), channel_id=1, source_target_pairs={{0,4},{1,5},{2,6},{3,7},{4,0},{5,1},{6,2},{7,3},{8,12},{9,13},{10,... | collective-permute-start | bytes 393224 | tf_op jit(solution)/shard_map/ppermute | solution.py:373
  21.4 3.0 %next_chunk.2 = (f32[128,512]{1,0:T(8,128)S(1)}, f32[128,512]{1,0:T(8,128)S(1)}, f32[128,512]{1,0:T(8,128)S(1)}, f32[128,512]{1,0:T(8,128)S(1)}) custom-call(bf16[1280,512]{1,0:T(8,128)(2,1)S(1)} %get-tuple-element.76.s0, bf16[1280,512]{1,0:T(8,128)(2,1)S(1)} %get-tuple-element.77.f0, bf16[1280,512]{1,0:T(8,128)(2,1)S(1)} %get-tuple-element.90.s1, ...), custom_call_target="tpu_custom_call" | custom-call | flops 1342177280 | bytes 1048576 | tf_op jit(solution)/shard_map/next_chunk/pallas_call | solution.py:341
  24.4 1.6 %collective-permute-start.8 = (f16[128,512]{1,0:T(8,128)(2,1)S(1)}, f16[128,512]{1,0:T(8,128)(2,1)S(1)}, u32[]{:S(2)}, u32[]{:S(2)}) collective-permute-start(f16[128,512]{1,0:T(8,128)(2,1)S(1)} %convert_element_type.83), channel_id=1, source_target_pairs={{0,2},{1,3},{2,0},{3,1},{4,6},{5,7},{6,4},{7,5},{8,10},{9,11},{10,... | collective-permute-start | bytes 393224 | tf_op jit(solution)/shard_map/ppermute | solution.py:373
  26.0 0.0 collective-permute-done.6
  26.0 0.7 %collective-permute-start.9 = (f16[128,512]{1,0:T(8,128)(2,1)S(1)}, f16[128,512]{1,0:T(8,128)(2,1)S(1)}, u32[]{:S(2)}, u32[]{:S(2)}) collective-permute-start(f16[128,512]{1,0:T(8,128)(2,1)S(1)} %add_convert_fusion.2), channel_id=1, source_target_pairs={{0,4},{1,5},{2,6},{3,7},{4,0},{5,1},{6,2},{7,3},{8,12},{9,13},{10,... | collective-permute-start | bytes 393224 | tf_op jit(solution)/shard_map/ppermute | solution.py:373
  26.7 1.6 %next_chunk.3 = (f32[128,512]{1,0:T(8,128)S(1)}, f32[128,512]{1,0:T(8,128)S(1)}) custom-call(bf16[1280,512]{1,0:T(8,128)(2,1)S(1)} %get-tuple-element.76.s0, bf16[1280,512]{1,0:T(8,128)(2,1)S(1)} %get-tuple-element.77.f0, bf16[1280,512]{1,0:T(8,128)(2,1)S(1)} %get-tuple-element.90.s1, bf16[1280,512]{1,0:T(8,128)(2,1)S(1)} %get-tuple-element.91.f1, ...), custom_call_target="tpu_custom_call" | custom-call | flops 671088640 | bytes 524288 | tf_op jit(solution)/shard_map/next_chunk/pallas_call | solution.py:341
  28.4 0.0 collective-permute-done.7
  28.4 1.1 %collective-permute-start.11 = (f16[128,512]{1,0:T(8,128)(2,1)S(1)}, f16[128,512]{1,0:T(8,128)(2,1)S(1)}, u32[]{:S(2)}, u32[]{:S(2)}) collective-permute-start(f16[128,512]{1,0:T(8,128)(2,1)S(1)} %add_convert_fusion.1), channel_id=1, source_target_pairs={{0,2},{1,3},{2,0},{3,1},{4,6},{5,7},{6,4},{7,5},{8,10},{9,11},{10,... | collective-permute-start | bytes 393224 | tf_op jit(solution)/shard_map/ppermute | solution.py:373
  29.6 0.9 %collective-permute-start.10 = (f16[128,512]{1,0:T(8,128)(2,1)S(1)}, f16[128,512]{1,0:T(8,128)(2,1)S(1)}, u32[]{:S(2)}, u32[]{:S(2)}) collective-permute-start(f16[128,512]{1,0:T(8,128)(2,1)S(1)} %convert_element_type.86), channel_id=1, source_target_pairs={{0,4},{1,5},{2,6},{3,7},{4,0},{5,1},{6,2},{7,3},{8,12},{9,13},{10,... | collective-permute-start | bytes 393224 | tf_op jit(solution)/shard_map/ppermute | solution.py:373
  30.5 0.0 collective-permute-done.8
  30.5 0.7 %collective-permute-done.9 = f16[128,512]{1,0:T(8,128)(2,1)S(1)} collective-permute-done((f16[128,512]{1,0:T(8,128)(2,1)S(1)}, f16[128,512]{1,0:T(8,128)(2,1)S(1)}, u32[]{:S(2)}, u32[]{:S(2)}) %collective-permute-start.9) | collective-permute-done | bytes 131104 | tf_op jit(solution)/shard_map/ppermute | solution.py:373
  31.2 0.1 add_convert_fusion
  31.2 2.7 %collective-permute-start.13 = (f16[64,512]{1,0:T(8,128)(2,1)S(1)}, f16[64,512]{1,0:T(8,128)(2,1)S(1)}, u32[]{:S(2)}, u32[]{:S(2)}) collective-permute-start(f16[64,512]{1,0:T(8,128)(2,1)S(1)} %get-tuple-element.99), channel_id=1, source_target_pairs={{0,16},{8,24},{16,0},{24,8},{1,17},{9,25},{17,1},{25,9},{2,18},{10... | collective-permute-start | bytes 196616 | tf_op jit(solution)/shard_map/ppermute | solution.py:378
  33.9 1.3 %collective-permute-start.14 = (f16[64,512]{1,0:T(8,128)(2,1)S(1)}, f16[64,512]{1,0:T(8,128)(2,1)S(1)}, u32[]{:S(2)}, u32[]{:S(2)}) collective-permute-start(f16[64,512]{1,0:T(8,128)(2,1)S(1)} %get-tuple-element.100), channel_id=1, source_target_pairs={{0,24},{8,16},{16,8},{24,0},{1,25},{9,17},{17,9},{25,1},{2,26},{10... | collective-permute-start | bytes 196616 | tf_op jit(solution)/shard_map/ppermute | solution.py:378
  35.3 0.0 collective-permute-done.11
  35.3 0.0 collective-permute-done.10
  35.3 0.1 convert_add_fusion
  35.3 0.9 %collective-permute-start.12 = (f16[64,512]{1,0:T(8,128)(2,1)S(1)}, f16[64,512]{1,0:T(8,128)(2,1)S(1)}, u32[]{:S(2)}, u32[]{:S(2)}) collective-permute-start(f16[64,512]{1,0:T(8,128)(2,1)S(1)} %slice_convert_fusion), channel_id=1, source_target_pairs={{0,8},{8,0},{16,24},{24,16},{1,9},{9,1},{17,25},{25,17},{2,10},{10... | collective-permute-start | bytes 196616 | tf_op jit(solution)/shard_map/ppermute | solution.py:378
  36.3 2.1 %collective-permute-done.13 = f16[64,512]{1,0:T(8,128)(2,1)S(1)} collective-permute-done((f16[64,512]{1,0:T(8,128)(2,1)S(1)}, f16[64,512]{1,0:T(8,128)(2,1)S(1)}, u32[]{:S(2)}, u32[]{:S(2)}) %collective-permute-start.13) | collective-permute-done | bytes 65568 | tf_op jit(solution)/shard_map/ppermute | solution.py:378
  38.4 1.7 %collective-permute-done.14 = f16[64,512]{1,0:T(8,128)(2,1)S(1)} collective-permute-done((f16[64,512]{1,0:T(8,128)(2,1)S(1)}, f16[64,512]{1,0:T(8,128)(2,1)S(1)}, u32[]{:S(2)}, u32[]{:S(2)}) %collective-permute-start.14) | collective-permute-done | bytes 65568 | tf_op jit(solution)/shard_map/ppermute | solution.py:378
  40.1 0.3 collective-permute-done.12
  40.4 0.7 %fusion.1 = f32[64,512]{1,0:T(8,128)} fusion(f32[64,512]{1,0:T(8,128)S(1)} %get-tuple-element.68, f32[64,512]{1,0:T(8,128)S(1)} %convert_add_fusion.1, f32[128,512]{1,0:T(8,128)S(1)} %convert_add_fusion, f16[64,512]{1,0:T(8,128)(2,1)S(1)} %collective-permute-done.12), kind=kLoop, calls=%fused_computation.8 | loop fusion | flops 131072 | bytes 589824 | tf_op jit(solution)/shard_map/mul | solution.py:486
  (17 shorter events, 0.4 us)
Async XLA Ops:
  0.0 9.6 %copy-start.2 = (f32[2048]{0:T(1024)S(1)}, f32[2048]{0:T(1024)}, u32[]{:S(2)}) copy-start(f32[2048]{0:T(1024)} %param.10) | copy-start | bytes 24580
  0.0 9.6 %copy-start.3 = (f32[2048]{0:T(1024)S(1)}, f32[2048]{0:T(1024)}, u32[]{:S(2)}) copy-start(f32[2048]{0:T(1024)} %param.11) | copy-start | bytes 24580
  3.3 1.5 %collective-permute-start = (f32[2,40,512]{2,1,0:T(8,128)S(1)}, f32[2,40,512]{2,1,0:T(8,128)S(1)}, u32[]{:S(2)}, u32[]{:S(2)}) collective-permute-start(f32[2,40,512]{2,1,0:T(8,128)S(1)} %get-tuple-element.54), channel_id=1, source_target_pairs={{0,1},{1,0},{2,3},{3,2},{4,5},{5,4},{6,7},{7,6},{8,9},{9,8},{10,11... | collective-permute-start | bytes 491528 | tf_op jit(solution)/shard_map/ppermute | solution.py:370
  5.0 11.2 %collective-permute-start.4 = (bf16[80,16,512]{2,1,0:T(8,128)(2,1)}, bf16[80,16,512]{2,1,0:T(8,128)(2,1)S(1)}, u32[]{:S(2)}, u32[]{:S(2)}) collective-permute-start(bf16[80,16,512]{2,1,0:T(8,128)(2,1)} %get-tuple-element.57.own), channel_id=1, source_target_pairs={{0,1},{1,0},{2,3},{3,2},{4,5},{5,4},{6,7},{7,6},{8,9},{9,8},{10,11... | collective-permute-start | bytes 3932168 | tf_op jit(solution)/shard_map/ppermute | solution.py:370
  5.4 6.5 %collective-permute-start.3 = (f16[3,40,512]{2,1,0:T(8,128)(2,1)S(1)}, f16[3,40,512]{2,1,0:T(8,128)(2,1)S(1)}, u32[]{:S(2)}, u32[]{:S(2)}) collective-permute-start(f16[3,40,512]{2,1,0:T(8,128)(2,1)S(1)} %pad_maximum_fusion.1), channel_id=1, source_target_pairs={{0,2},{1,3},{2,0},{3,1},{4,6},{5,7},{6,4},{7,5},{8,10},{9,11},{10,... | collective-permute-start | bytes 368648 | tf_op jit(solution)/shard_map/ppermute | solution.py:373
  8.1 7.9 %collective-permute-start.2 = (f16[3,40,512]{2,1,0:T(8,128)(2,1)S(1)}, f16[3,40,512]{2,1,0:T(8,128)(2,1)S(1)}, u32[]{:S(2)}, u32[]{:S(2)}) collective-permute-start(f16[3,40,512]{2,1,0:T(8,128)(2,1)S(1)} %pad_maximum_fusion.1), channel_id=1, source_target_pairs={{0,4},{1,5},{2,6},{3,7},{4,0},{5,1},{6,2},{7,3},{8,12},{9,13},{10,... | collective-permute-start | bytes 368648 | tf_op jit(solution)/shard_map/ppermute | solution.py:373
  9.6 6.4 %collective-permute-start.1 = (f16[3,40,512]{2,1,0:T(8,128)(2,1)S(1)}, f16[3,40,512]{2,1,0:T(8,128)(2,1)S(1)}, u32[]{:S(2)}, u32[]{:S(2)}) collective-permute-start(f16[3,40,512]{2,1,0:T(8,128)(2,1)S(1)} %pad_maximum_fusion.1), channel_id=1, source_target_pairs={{0,6},{1,7},{2,4},{3,5},{4,2},{5,3},{6,0},{7,1},{8,14},{9,15},{10,... | collective-permute-start | bytes 368648 | tf_op jit(solution)/shard_map/ppermute | solution.py:373
  11.9 4.4 %copy-start = (bf16[80,16,512]{2,1,0:T(8,128)(2,1)S(1)}, bf16[80,16,512]{2,1,0:T(8,128)(2,1)}, u32[]{:S(2)}) copy-start(bf16[80,16,512]{2,1,0:T(8,128)(2,1)} %get-tuple-element.57.own) | copy-start | bytes 3932164
  11.9 4.4 %copy-start.1 = (f32[512]{0:T(512)S(1)}, f32[512]{0:T(512)}, u32[]{:S(2)}) copy-start(f32[512]{0:T(512)} %param.12) | copy-start | bytes 6148
  16.2 1.5 %collective-permute-start.5 = (f32[2,40,512]{2,1,0:T(8,128)S(1)}, f32[2,40,512]{2,1,0:T(8,128)S(1)}, u32[]{:S(2)}, u32[]{:S(2)}) collective-permute-start(f32[2,40,512]{2,1,0:T(8,128)S(1)} %pad_maximum_fusion.stats), channel_id=1, source_target_pairs={{0,1},{1,0},{2,3},{3,2},{4,5},{5,4},{6,7},{7,6},{8,9},{9,8},{10,11... | collective-permute-start | bytes 491528 | tf_op jit(solution)/shard_map/ppermute | solution.py:370
  19.2 6.8 %collective-permute-start.6 = (f16[128,512]{1,0:T(8,128)(2,1)S(1)}, f16[128,512]{1,0:T(8,128)(2,1)S(1)}, u32[]{:S(2)}, u32[]{:S(2)}) collective-permute-start(f16[128,512]{1,0:T(8,128)(2,1)S(1)} %convert_element_type.82), channel_id=1, source_target_pairs={{0,2},{1,3},{2,0},{3,1},{4,6},{5,7},{6,4},{7,5},{8,10},{9,11},{10,... | collective-permute-start | bytes 393224 | tf_op jit(solution)/shard_map/ppermute | solution.py:373
  20.5 7.9 %collective-permute-start.7 = (f16[128,512]{1,0:T(8,128)(2,1)S(1)}, f16[128,512]{1,0:T(8,128)(2,1)S(1)}, u32[]{:S(2)}, u32[]{:S(2)}) collective-permute-start(f16[128,512]{1,0:T(8,128)(2,1)S(1)} %convert_element_type.81), channel_id=1, source_target_pairs={{0,4},{1,5},{2,6},{3,7},{4,0},{5,1},{6,2},{7,3},{8,12},{9,13},{10,... | collective-permute-start | bytes 393224 | tf_op jit(solution)/shard_map/ppermute | solution.py:373
  24.4 6.0 %collective-permute-start.8 = (f16[128,512]{1,0:T(8,128)(2,1)S(1)}, f16[128,512]{1,0:T(8,128)(2,1)S(1)}, u32[]{:S(2)}, u32[]{:S(2)}) collective-permute-start(f16[128,512]{1,0:T(8,128)(2,1)S(1)} %convert_element_type.83), channel_id=1, source_target_pairs={{0,2},{1,3},{2,0},{3,1},{4,6},{5,7},{6,4},{7,5},{8,10},{9,11},{10,... | collective-permute-start | bytes 393224 | tf_op jit(solution)/shard_map/ppermute | solution.py:373
  26.0 5.1 %collective-permute-start.9 = (f16[128,512]{1,0:T(8,128)(2,1)S(1)}, f16[128,512]{1,0:T(8,128)(2,1)S(1)}, u32[]{:S(2)}, u32[]{:S(2)}) collective-permute-start(f16[128,512]{1,0:T(8,128)(2,1)S(1)} %add_convert_fusion.2), channel_id=1, source_target_pairs={{0,4},{1,5},{2,6},{3,7},{4,0},{5,1},{6,2},{7,3},{8,12},{9,13},{10,... | collective-permute-start | bytes 393224 | tf_op jit(solution)/shard_map/ppermute | solution.py:373
  28.4 6.8 %collective-permute-start.11 = (f16[128,512]{1,0:T(8,128)(2,1)S(1)}, f16[128,512]{1,0:T(8,128)(2,1)S(1)}, u32[]{:S(2)}, u32[]{:S(2)}) collective-permute-start(f16[128,512]{1,0:T(8,128)(2,1)S(1)} %add_convert_fusion.1), channel_id=1, source_target_pairs={{0,2},{1,3},{2,0},{3,1},{4,6},{5,7},{6,4},{7,5},{8,10},{9,11},{10,... | collective-permute-start | bytes 393224 | tf_op jit(solution)/shard_map/ppermute | solution.py:373
  29.6 5.7 %collective-permute-start.10 = (f16[128,512]{1,0:T(8,128)(2,1)S(1)}, f16[128,512]{1,0:T(8,128)(2,1)S(1)}, u32[]{:S(2)}, u32[]{:S(2)}) collective-permute-start(f16[128,512]{1,0:T(8,128)(2,1)S(1)} %convert_element_type.86), channel_id=1, source_target_pairs={{0,4},{1,5},{2,6},{3,7},{4,0},{5,1},{6,2},{7,3},{8,12},{9,13},{10,... | collective-permute-start | bytes 393224 | tf_op jit(solution)/shard_map/ppermute | solution.py:373
  31.2 7.2 %collective-permute-start.13 = (f16[64,512]{1,0:T(8,128)(2,1)S(1)}, f16[64,512]{1,0:T(8,128)(2,1)S(1)}, u32[]{:S(2)}, u32[]{:S(2)}) collective-permute-start(f16[64,512]{1,0:T(8,128)(2,1)S(1)} %get-tuple-element.99), channel_id=1, source_target_pairs={{0,16},{8,24},{16,0},{24,8},{1,17},{9,25},{17,1},{25,9},{2,18},{10... | collective-permute-start | bytes 196616 | tf_op jit(solution)/shard_map/ppermute | solution.py:378
  33.9 6.2 %collective-permute-start.14 = (f16[64,512]{1,0:T(8,128)(2,1)S(1)}, f16[64,512]{1,0:T(8,128)(2,1)S(1)}, u32[]{:S(2)}, u32[]{:S(2)}) collective-permute-start(f16[64,512]{1,0:T(8,128)(2,1)S(1)} %get-tuple-element.100), channel_id=1, source_target_pairs={{0,24},{8,16},{16,8},{24,0},{1,25},{9,17},{17,9},{25,1},{2,26},{10... | collective-permute-start | bytes 196616 | tf_op jit(solution)/shard_map/ppermute | solution.py:378
  35.3 5.0 %collective-permute-start.12 = (f16[64,512]{1,0:T(8,128)(2,1)S(1)}, f16[64,512]{1,0:T(8,128)(2,1)S(1)}, u32[]{:S(2)}, u32[]{:S(2)}) collective-permute-start(f16[64,512]{1,0:T(8,128)(2,1)S(1)} %slice_convert_fusion), channel_id=1, source_target_pairs={{0,8},{8,0},{16,24},{24,16},{1,9},{9,1},{17,25},{25,17},{2,10},{10... | collective-permute-start | bytes 196616 | tf_op jit(solution)/shard_map/ppermute | solution.py:378
where the time goes:
time: 41.3 us; the launch traced here: 41.1 us
  starting transfers between devices  16.6 us (40%)
  Pallas kernels  12.9 us (31%)
  waiting for transfers between devices  10 us (24%)
  other arithmetic  1.28 us (3%)
    ppermute x9, starting transfers between devices, to_chip(): lax.ppermute(x, 'inner', [(i, partner(i // 2, d) * 2 + i % 2) for i in ra...  10.6 us
    ppermute x3, starting transfers between devices, to_group(): return lax.ppermute(x, 'outer', [(g, beyond(g, s)) for g in range(groups)])  4.95 us
    ppermute x9, waiting for transfers between devices, to_chip(): lax.ppermute(x, 'inner', [(i, partner(i // 2, d) * 2 + i % 2) for i in ra...  4.94 us
    pallas_call x2, Pallas kernels, next_chunk(): pl.pallas_call(functools.partial(next_kernel, tile), in_specs=[VMEM] * 6,...  4.66 us
    ppermute x3, waiting for transfers between devices, to_group(): return lax.ppermute(x, 'outer', [(g, beyond(g, s)) for g in range(groups)])  4.07 us
    pallas_call x1, Pallas kernels, gather_nodes(): pl.pallas_call(functools.partial(gather_kernel, part), in_specs=[HBM, HBM...  3.32 us
    pallas_call x1, Pallas kernels, order(): pl.pallas_call(functools.partial(order_kernel, unit, bound, plan, far), i...  2.12 us
    pallas_call x1, Pallas kernels, first_chunk(): pl.pallas_call(first_kernel, in_specs=[VMEM] * 8, out_specs=[VMEM] * (2 +...  1.39 us
  transfers between devices with their start and end apart: 15, of which 7 were waited for; matrix products, arithmetic and copies ran while one was open for 1% of the time, Pallas kernels for 20%

commit v1 on v0

--- a/solution.py
+++ b/solution.py
@@ -145,7 +145,7 @@
     blocks, copies = [], []
     for k, (chunk, step) in enumerate(cells):
         d, away = plan[chunk][step]
-        to_chip, to_group = far(chip, d, group, away)
+        to_chip, to_group = far(chip, core, d, group, away)
         block = (to_group * (lax.axis_size("inner") // 2) + to_chip) * 2 + core
         copy = pltpu.make_async_copy(loadings_hbm.at[block], own.at[k], sems.at[k])
         copy.start()
@@ -360,7 +360,11 @@
     rows = instruments // (groups * inner)
     paired = chips & (chips - 1) == 0
 
-    def partner(of, d):
+    relayed = chips == 4 and groups % 2 == 0
+
+    def partner(of, core, d):
+        if relayed and d in (1, 2):
+            d = d + (3 - 2 * d) * core
         return of ^ d if paired else (of + d) % chips
 
     def beyond(of, s):
@@ -371,7 +375,7 @@
 
     def to_chip(x, d):
         return lax.ppermute(
-            x, "inner", [(i, partner(i // 2, d) * 2 + i % 2) for i in range(inner)]
+            x, "inner", [(i, partner(i // 2, i % 2, d) * 2 + i % 2) for i in range(inner)]
         )
 
     def to_group(x, s):
@@ -406,7 +410,6 @@
             message = to_message(sums, within)
     theirs = to_core(chosen)
     steps = range(groups)
-    relayed = chips == 4 and groups % 2 == 0
     if relayed:
         half = groups // 2
         low, high = steps[:half], steps[half:]
@@ -419,7 +422,7 @@
     else:
         plan = [[(d, s) for s in steps] for d in range(chips - 1, -1, -1)]
         first_sizes = (groups * rows,)
-    far = lambda chip, d, group, s: (partner(chip, d), beyond(group, s))
+    far = lambda chip, core, d, group, s: (partner(chip, core, d), beyond(group, s))
     levels, live, gain, *parts = order(
         unit, bound, plan, far, tail, states, loadings, strikes, hedge
     )

time: 41.3 us -> 41.6 us (level)
  transfers between devices with their start and end apart: 15 -> 15, of which waited for: 7 -> 8; matrix products, arithmetic and copies ran while one was open for 1% -> 1% of each run, Pallas kernels for 20% -> 20%
where the time goes in v1:
time: 41.6 us; the launch traced here: 41.3 us
  starting transfers between devices  17 us (41%)
  Pallas kernels  12.9 us (31%)
  waiting for transfers between devices  9.85 us (24%)
  other arithmetic  1.28 us (3%)
    ppermute x9, starting transfers between devices, to_chip(): lax.ppermute(x, 'inner', [(i, partner(i // 2, i % 2, d) * 2 + i % 2) for...  11 us
    ppermute x3, starting transfers between devices, to_group(): return lax.ppermute(x, 'outer', [(g, beyond(g, s)) for g in range(groups)])  5 us
    ppermute x9, waiting for transfers between devices, to_chip(): lax.ppermute(x, 'inner', [(i, partner(i // 2, i % 2, d) * 2 + i % 2) for...  4.74 us
    pallas_call x2, Pallas kernels, next_chunk(): pl.pallas_call(functools.partial(next_kernel, tile), in_specs=[VMEM] * 6,...  4.66 us
    ppermute x3, waiting for transfers between devices, to_group(): return lax.ppermute(x, 'outer', [(g, beyond(g, s)) for g in range(groups)])  4.07 us
    pallas_call x1, Pallas kernels, gather_nodes(): pl.pallas_call(functools.partial(gather_kernel, part), in_specs=[HBM, HBM...  3.32 us
    pallas_call x1, Pallas kernels, order(): pl.pallas_call(functools.partial(order_kernel, unit, bound, plan, far), i...  2.11 us
    pallas_call x1, Pallas kernels, ready_rows(): pl.pallas_call(ready_kernel, in_specs=[VMEM] * 7, out_specs=[VMEM] * 3, o...  1.39 us
  transfers between devices with their start and end apart: 15, of which 8 were waited for; matrix products, arithmetic and copies ran while one was open for 1% of the time, Pallas kernels for 20%

profile of v1, /device:TPU:0, one launch (start us, length us, event | category | flops | bytes accessed | tf_op | source)
XLA Modules:
  0.0 41.3 jit_solution(5544432934592890523)
XLA Ops:
  0.0 0.0 copy-start.2
  0.0 0.0 copy-start.3
  0.0 3.3 %gather_nodes.1 = (bf16[80,16,512]{2,1,0:T(8,128)(2,1)}, f32[2,40,512]{2,1,0:T(8,128)S(1)}, f32[2,40,512]{2,1,0:T(8,128)S(1)}) custom-call(s32[128]{0:T(128)} %tail_hbm.3, bf16[128,16,512]{2,1,0:T(8,128)(2,1)} %normals.1), custom_call_target="tpu_custom_call" | custom-call | tf_op jit(solution)/shard_map/gather_nodes/pallas_call | solution.py:91
  3.3 0.5 %collective-permute-start = (f32[2,40,512]{2,1,0:T(8,128)S(1)}, f32[2,40,512]{2,1,0:T(8,128)S(1)}, u32[]{:S(2)}, u32[]{:S(2)}) collective-permute-start(f32[2,40,512]{2,1,0:T(8,128)S(1)} %get-tuple-element.54), channel_id=1, source_target_pairs={{0,1},{1,0},{2,3},{3,2},{4,5},{5,4},{6,7},{7,6},{8,9},{9,8},{10,11... | collective-permute-start | bytes 491528 | tf_op jit(solution)/shard_map/ppermute | solution.py:374
  3.8 1.0 %collective-permute-done = f32[2,40,512]{2,1,0:T(8,128)S(1)} collective-permute-done((f32[2,40,512]{2,1,0:T(8,128)S(1)}, f32[2,40,512]{2,1,0:T(8,128)S(1)}, u32[]{:S(2)}, u32[]{:S(2)}) %collective-permute-start) | collective-permute-done | bytes 163872 | tf_op jit(solution)/shard_map/ppermute | solution.py:374
  5.0 0.4 %collective-permute-start.4 = (bf16[80,16,512]{2,1,0:T(8,128)(2,1)}, bf16[80,16,512]{2,1,0:T(8,128)(2,1)S(1)}, u32[]{:S(2)}, u32[]{:S(2)}) collective-permute-start(bf16[80,16,512]{2,1,0:T(8,128)(2,1)} %get-tuple-element.57.own), channel_id=1, source_target_pairs={{0,1},{1,0},{2,3},{3,2},{4,5},{5,4},{6,7},{7,6},{8,9},{9,8},{10,11... | collective-permute-start | bytes 3932168 | tf_op jit(solution)/shard_map/ppermute | solution.py:374
  5.4 2.6 %collective-permute-start.3 = (f16[3,40,512]{2,1,0:T(8,128)(2,1)S(1)}, f16[3,40,512]{2,1,0:T(8,128)(2,1)S(1)}, u32[]{:S(2)}, u32[]{:S(2)}) collective-permute-start(f16[3,40,512]{2,1,0:T(8,128)(2,1)S(1)} %pad_maximum_fusion.1), channel_id=1, source_target_pairs={{0,2},{1,5},{2,0},{3,7},{4,6},{5,1},{6,4},{7,3},{8,10},{9,13},{10,... | collective-permute-start | bytes 368648 | tf_op jit(solution)/shard_map/ppermute | solution.py:377
  8.0 1.5 %collective-permute-start.2 = (f16[3,40,512]{2,1,0:T(8,128)(2,1)S(1)}, f16[3,40,512]{2,1,0:T(8,128)(2,1)S(1)}, u32[]{:S(2)}, u32[]{:S(2)}) collective-permute-start(f16[3,40,512]{2,1,0:T(8,128)(2,1)S(1)} %pad_maximum_fusion.1), channel_id=1, source_target_pairs={{0,4},{1,3},{2,6},{3,1},{4,0},{5,7},{6,2},{7,5},{8,12},{9,11},{10,... | collective-permute-start | bytes 368648 | tf_op jit(solution)/shard_map/ppermute | solution.py:377
  9.6 0.0 collective-permute-start.1
  9.6 0.0 copy-done.2
  9.6 0.0 copy-done.3
  9.6 2.1 %order_instruments.1 = (f32[80,512]{1,0:T(8,128)S(1)}, f32[40,512]{1,0:T(8,128)S(1)}, f32[64,512]{1,0:T(8,128)S(1)}, bf16[4,64,512]{2,1,0:T(8,128)(2,1)S(1)}, bf...) custom-call(s32[128]{0:T(128)} %tail_hbm.3, ...), custom_call_target="tpu_custom_call" | custom-call | bytes 1048576 | tf_op jit(solution)/shard_map/order_instruments/pallas_call | solution.py:201
  11.7 0.0 collective-permute-done.3
  11.7 0.0 copy-start
  11.7 0.0 copy-start.1
  11.8 2.8 %collective-permute-done.2 = f16[3,40,512]{2,1,0:T(8,128)(2,1)S(1)} collective-permute-done((f16[3,40,512]{2,1,0:T(8,128)(2,1)S(1)}, f16[3,40,512]{2,1,0:T(8,128)(2,1)S(1)}, u32[]{:S(2)}, u32[]{:S(2)}) %collective-permute-start.2) | collective-permute-done | bytes 122912 | tf_op jit(solution)/shard_map/ppermute | solution.py:377
  14.6 1.1 %collective-permute-done.1 = f16[3,40,512]{2,1,0:T(8,128)(2,1)S(1)} collective-permute-done((f16[3,40,512]{2,1,0:T(8,128)(2,1)S(1)}, f16[3,40,512]{2,1,0:T(8,128)(2,1)S(1)}, u32[]{:S(2)}, u32[]{:S(2)}) %collective-permute-start.1) | collective-permute-done | bytes 122912 | tf_op jit(solution)/shard_map/ppermute | solution.py:377
  15.8 0.1 fusion.3
  15.9 0.0 collective-permute-done.4.theirs
  15.9 0.1 collective-permute-start.5
  16.0 0.0 copy-done
  16.0 0.0 copy-done.1
  16.0 1.4 %ready_rows.1 = (bf16[1280,512]{1,0:T(8,128)(2,1)S(1)}, bf16[1280,512]{1,0:T(8,128)(2,1)S(1)}, f32[256,512]{1,0:T(8,128)S(1)}) custom-call(bf16[80,16,512]{2,1,0:T(8,128)(2,1)S(1)} %copy-done, bf16[80,16,512]{2,1,0:T(8,128)(2,1)S(1)} %collective-permute-done.4.theirs, f32[2,40,512]{2,1,0:T(8,128)S(1)} %pad_maximum_fusion.stats, ...), custom_call_target="tpu_custom_call" | custom-call | flops 335544320 | bytes 524288 | tf_op jit(solution)/shard_map/ready_rows/pallas_call | solution.py:255
  17.4 0.0 collective-permute-done.5.stats
  17.5 1.4 %first_chunk.1 = (bf16[1280,512]{1,0:T(8,128)(2,1)S(1)}, bf16[1280,512]{1,0:T(8,128)(2,1)S(1)}, f32[128,512]{1,0:T(8,128)S(1)}, f32[128,512]{1,0:T(8,128)S(1)}) custom-call(bf16[80,16,512]{2,1,0:T(8,128)(2,1)S(1)} %copy-done, bf16[80,16,512]{2,1,0:T(8,128)(2,1)S(1)} %collective-permute-done.4.theirs, f32[2,40,512]{2,1,0:T(8,128)S(1)} %collective-permute-done.5.stats, ...), custom_call_target="tpu_custom_call" | custom-call | flops 335544320 | bytes 524288 | tf_op jit(solution)/shard_map/first_chunk/pallas_call | solution.py:327
  18.9 1.8 %collective-permute-start.6 = (f16[128,512]{1,0:T(8,128)(2,1)S(1)}, f16[128,512]{1,0:T(8,128)(2,1)S(1)}, u32[]{:S(2)}, u32[]{:S(2)}) collective-permute-start(f16[128,512]{1,0:T(8,128)(2,1)S(1)} %convert_element_type.82), channel_id=1, source_target_pairs={{0,2},{1,5},{2,0},{3,7},{4,6},{5,1},{6,4},{7,3},{8,10},{9,13},{10,... | collective-permute-start | bytes 393224 | tf_op jit(solution)/shard_map/ppermute | solution.py:377
  20.7 0.7 %collective-permute-start.7 = (f16[128,512]{1,0:T(8,128)(2,1)S(1)}, f16[128,512]{1,0:T(8,128)(2,1)S(1)}, u32[]{:S(2)}, u32[]{:S(2)}) collective-permute-start(f16[128,512]{1,0:T(8,128)(2,1)S(1)} %convert_element_type.81), channel_id=1, source_target_pairs={{0,4},{1,3},{2,6},{3,1},{4,0},{5,7},{6,2},{7,5},{8,12},{9,11},{10,... | collective-permute-start | bytes 393224 | tf_op jit(solution)/shard_map/ppermute | solution.py:377
  21.4 3.0 %next_chunk.2 = (f32[128,512]{1,0:T(8,128)S(1)}, f32[128,512]{1,0:T(8,128)S(1)}, f32[128,512]{1,0:T(8,128)S(1)}, f32[128,512]{1,0:T(8,128)S(1)}) custom-call(bf16[1280,512]{1,0:T(8,128)(2,1)S(1)} %get-tuple-element.76.s0, bf16[1280,512]{1,0:T(8,128)(2,1)S(1)} %get-tuple-element.77.f0, bf16[1280,512]{1,0:T(8,128)(2,1)S(1)} %get-tuple-element.90.s1, ...), custom_call_target="tpu_custom_call" | custom-call | flops 1342177280 | bytes 1048576 | tf_op jit(solution)/shard_map/next_chunk/pallas_call | solution.py:341
  24.5 1.1 %collective-permute-start.8 = (f16[128,512]{1,0:T(8,128)(2,1)S(1)}, f16[128,512]{1,0:T(8,128)(2,1)S(1)}, u32[]{:S(2)}, u32[]{:S(2)}) collective-permute-start(f16[128,512]{1,0:T(8,128)(2,1)S(1)} %convert_element_type.83), channel_id=1, source_target_pairs={{0,2},{1,5},{2,0},{3,7},{4,6},{5,1},{6,4},{7,3},{8,10},{9,13},{10,... | collective-permute-start | bytes 393224 | tf_op jit(solution)/shard_map/ppermute | solution.py:377
  25.6 0.0 collective-permute-done.6
  25.6 1.1 %collective-permute-start.9 = (f16[128,512]{1,0:T(8,128)(2,1)S(1)}, f16[128,512]{1,0:T(8,128)(2,1)S(1)}, u32[]{:S(2)}, u32[]{:S(2)}) collective-permute-start(f16[128,512]{1,0:T(8,128)(2,1)S(1)} %add_convert_fusion.2), channel_id=1, source_target_pairs={{0,4},{1,3},{2,6},{3,1},{4,0},{5,7},{6,2},{7,5},{8,12},{9,11},{10,... | collective-permute-start | bytes 393224 | tf_op jit(solution)/shard_map/ppermute | solution.py:377
  26.8 1.6 %next_chunk.3 = (f32[128,512]{1,0:T(8,128)S(1)}, f32[128,512]{1,0:T(8,128)S(1)}) custom-call(bf16[1280,512]{1,0:T(8,128)(2,1)S(1)} %get-tuple-element.76.s0, bf16[1280,512]{1,0:T(8,128)(2,1)S(1)} %get-tuple-element.77.f0, bf16[1280,512]{1,0:T(8,128)(2,1)S(1)} %get-tuple-element.90.s1, bf16[1280,512]{1,0:T(8,128)(2,1)S(1)} %get-tuple-element.91.f1, ...), custom_call_target="tpu_custom_call" | custom-call | flops 671088640 | bytes 524288 | tf_op jit(solution)/shard_map/next_chunk/pallas_call | solution.py:341
  28.4 0.0 collective-permute-done.7
  28.5 1.4 %collective-permute-start.11 = (f16[128,512]{1,0:T(8,128)(2,1)S(1)}, f16[128,512]{1,0:T(8,128)(2,1)S(1)}, u32[]{:S(2)}, u32[]{:S(2)}) collective-permute-start(f16[128,512]{1,0:T(8,128)(2,1)S(1)} %add_convert_fusion.1), channel_id=1, source_target_pairs={{0,2},{1,5},{2,0},{3,7},{4,6},{5,1},{6,4},{7,3},{8,10},{9,13},{10,... | collective-permute-start | bytes 393224 | tf_op jit(solution)/shard_map/ppermute | solution.py:377
  29.8 0.7 %collective-permute-start.10 = (f16[128,512]{1,0:T(8,128)(2,1)S(1)}, f16[128,512]{1,0:T(8,128)(2,1)S(1)}, u32[]{:S(2)}, u32[]{:S(2)}) collective-permute-start(f16[128,512]{1,0:T(8,128)(2,1)S(1)} %convert_element_type.86), channel_id=1, source_target_pairs={{0,4},{1,3},{2,6},{3,1},{4,0},{5,7},{6,2},{7,5},{8,12},{9,11},{10,... | collective-permute-start | bytes 393224 | tf_op jit(solution)/shard_map/ppermute | solution.py:377
  30.6 0.3 collective-permute-done.8
  30.8 0.5 %collective-permute-done.9 = f16[128,512]{1,0:T(8,128)(2,1)S(1)} collective-permute-done((f16[128,512]{1,0:T(8,128)(2,1)S(1)}, f16[128,512]{1,0:T(8,128)(2,1)S(1)}, u32[]{:S(2)}, u32[]{:S(2)}) %collective-permute-start.9) | collective-permute-done | bytes 131104 | tf_op jit(solution)/shard_map/ppermute | solution.py:377
  31.3 0.1 add_convert_fusion
  31.4 2.3 %collective-permute-start.13 = (f16[64,512]{1,0:T(8,128)(2,1)S(1)}, f16[64,512]{1,0:T(8,128)(2,1)S(1)}, u32[]{:S(2)}, u32[]{:S(2)}) collective-permute-start(f16[64,512]{1,0:T(8,128)(2,1)S(1)} %get-tuple-element.99), channel_id=1, source_target_pairs={{0,16},{8,24},{16,0},{24,8},{1,17},{9,25},{17,1},{25,9},{2,18},{10... | collective-permute-start | bytes 196616 | tf_op jit(solution)/shard_map/ppermute | solution.py:382
  33.8 1.4 %collective-permute-start.14 = (f16[64,512]{1,0:T(8,128)(2,1)S(1)}, f16[64,512]{1,0:T(8,128)(2,1)S(1)}, u32[]{:S(2)}, u32[]{:S(2)}) collective-permute-start(f16[64,512]{1,0:T(8,128)(2,1)S(1)} %get-tuple-element.100), channel_id=1, source_target_pairs={{0,24},{8,16},{16,8},{24,0},{1,25},{9,17},{17,9},{25,1},{2,26},{10... | collective-permute-start | bytes 196616 | tf_op jit(solution)/shard_map/ppermute | solution.py:382
  35.1 0.0 collective-permute-done.11
  35.1 0.0 collective-permute-done.10
  35.1 0.1 convert_add_fusion
  35.2 1.3 %collective-permute-start.12 = (f16[64,512]{1,0:T(8,128)(2,1)S(1)}, f16[64,512]{1,0:T(8,128)(2,1)S(1)}, u32[]{:S(2)}, u32[]{:S(2)}) collective-permute-start(f16[64,512]{1,0:T(8,128)(2,1)S(1)} %slice_convert_fusion), channel_id=1, source_target_pairs={{0,8},{8,0},{16,24},{24,16},{1,9},{9,1},{17,25},{25,17},{2,10},{10... | collective-permute-start | bytes 196616 | tf_op jit(solution)/shard_map/ppermute | solution.py:382
  36.5 2.4 %collective-permute-done.13 = f16[64,512]{1,0:T(8,128)(2,1)S(1)} collective-permute-done((f16[64,512]{1,0:T(8,128)(2,1)S(1)}, f16[64,512]{1,0:T(8,128)(2,1)S(1)}, u32[]{:S(2)}, u32[]{:S(2)}) %collective-permute-start.13) | collective-permute-done | bytes 65568 | tf_op jit(solution)/shard_map/ppermute | solution.py:382
  39.0 1.1 %collective-permute-done.14 = f16[64,512]{1,0:T(8,128)(2,1)S(1)} collective-permute-done((f16[64,512]{1,0:T(8,128)(2,1)S(1)}, f16[64,512]{1,0:T(8,128)(2,1)S(1)}, u32[]{:S(2)}, u32[]{:S(2)}) %collective-permute-start.14) | collective-permute-done | bytes 65568 | tf_op jit(solution)/shard_map/ppermute | solution.py:382
  40.1 0.5 %collective-permute-done.12 = f16[64,512]{1,0:T(8,128)(2,1)S(1)} collective-permute-done((f16[64,512]{1,0:T(8,128)(2,1)S(1)}, f16[64,512]{1,0:T(8,128)(2,1)S(1)}, u32[]{:S(2)}, u32[]{:S(2)}) %collective-permute-start.12) | collective-permute-done | bytes 65568 | tf_op jit(solution)/shard_map/ppermute | solution.py:382
  40.6 0.7 %fusion.1 = f32[64,512]{1,0:T(8,128)} fusion(f32[64,512]{1,0:T(8,128)S(1)} %get-tuple-element.68, f32[64,512]{1,0:T(8,128)S(1)} %convert_add_fusion.1, f32[128,512]{1,0:T(8,128)S(1)} %convert_add_fusion, f16[64,512]{1,0:T(8,128)(2,1)S(1)} %collective-permute-done.12), kind=kLoop, calls=%fused_computation.8 | loop fusion | flops 131072 | bytes 589824 | tf_op jit(solution)/shard_map/mul | solution.py:489
  (17 shorter events, 0.4 us)
Async XLA Ops:
  0.0 9.6 %copy-start.2 = (f32[2048]{0:T(1024)S(1)}, f32[2048]{0:T(1024)}, u32[]{:S(2)}) copy-start(f32[2048]{0:T(1024)} %param.10) | copy-start | bytes 24580
  0.0 9.6 %copy-start.3 = (f32[2048]{0:T(1024)S(1)}, f32[2048]{0:T(1024)}, u32[]{:S(2)}) copy-start(f32[2048]{0:T(1024)} %param.11) | copy-start | bytes 24580
  3.3 1.5 %collective-permute-start = (f32[2,40,512]{2,1,0:T(8,128)S(1)}, f32[2,40,512]{2,1,0:T(8,128)S(1)}, u32[]{:S(2)}, u32[]{:S(2)}) collective-permute-start(f32[2,40,512]{2,1,0:T(8,128)S(1)} %get-tuple-element.54), channel_id=1, source_target_pairs={{0,1},{1,0},{2,3},{3,2},{4,5},{5,4},{6,7},{7,6},{8,9},{9,8},{10,11... | collective-permute-start | bytes 491528 | tf_op jit(solution)/shard_map/ppermute | solution.py:374
  5.0 10.9 %collective-permute-start.4 = (bf16[80,16,512]{2,1,0:T(8,128)(2,1)}, bf16[80,16,512]{2,1,0:T(8,128)(2,1)S(1)}, u32[]{:S(2)}, u32[]{:S(2)}) collective-permute-start(bf16[80,16,512]{2,1,0:T(8,128)(2,1)} %get-tuple-element.57.own), channel_id=1, source_target_pairs={{0,1},{1,0},{2,3},{3,2},{4,5},{5,4},{6,7},{7,6},{8,9},{9,8},{10,11... | collective-permute-start | bytes 3932168 | tf_op jit(solution)/shard_map/ppermute | solution.py:374
  5.4 6.3 %collective-permute-start.3 = (f16[3,40,512]{2,1,0:T(8,128)(2,1)S(1)}, f16[3,40,512]{2,1,0:T(8,128)(2,1)S(1)}, u32[]{:S(2)}, u32[]{:S(2)}) collective-permute-start(f16[3,40,512]{2,1,0:T(8,128)(2,1)S(1)} %pad_maximum_fusion.1), channel_id=1, source_target_pairs={{0,2},{1,5},{2,0},{3,7},{4,6},{5,1},{6,4},{7,3},{8,10},{9,13},{10,... | collective-permute-start | bytes 368648 | tf_op jit(solution)/shard_map/ppermute | solution.py:377
  8.0 6.6 %collective-permute-start.2 = (f16[3,40,512]{2,1,0:T(8,128)(2,1)S(1)}, f16[3,40,512]{2,1,0:T(8,128)(2,1)S(1)}, u32[]{:S(2)}, u32[]{:S(2)}) collective-permute-start(f16[3,40,512]{2,1,0:T(8,128)(2,1)S(1)} %pad_maximum_fusion.1), channel_id=1, source_target_pairs={{0,4},{1,3},{2,6},{3,1},{4,0},{5,7},{6,2},{7,5},{8,12},{9,11},{10,... | collective-permute-start | bytes 368648 | tf_op jit(solution)/shard_map/ppermute | solution.py:377
  9.6 6.2 %collective-permute-start.1 = (f16[3,40,512]{2,1,0:T(8,128)(2,1)S(1)}, f16[3,40,512]{2,1,0:T(8,128)(2,1)S(1)}, u32[]{:S(2)}, u32[]{:S(2)}) collective-permute-start(f16[3,40,512]{2,1,0:T(8,128)(2,1)S(1)} %pad_maximum_fusion.1), channel_id=1, source_target_pairs={{0,6},{1,7},{2,4},{3,5},{4,2},{5,3},{6,0},{7,1},{8,14},{9,15},{10,... | collective-permute-start | bytes 368648 | tf_op jit(solution)/shard_map/ppermute | solution.py:377
  11.7 4.3 %copy-start = (bf16[80,16,512]{2,1,0:T(8,128)(2,1)S(1)}, bf16[80,16,512]{2,1,0:T(8,128)(2,1)}, u32[]{:S(2)}) copy-start(bf16[80,16,512]{2,1,0:T(8,128)(2,1)} %get-tuple-element.57.own) | copy-start | bytes 3932164
  11.7 4.3 %copy-start.1 = (f32[512]{0:T(512)S(1)}, f32[512]{0:T(512)}, u32[]{:S(2)}) copy-start(f32[512]{0:T(512)} %param.12) | copy-start | bytes 6148
  15.9 1.5 %collective-permute-start.5 = (f32[2,40,512]{2,1,0:T(8,128)S(1)}, f32[2,40,512]{2,1,0:T(8,128)S(1)}, u32[]{:S(2)}, u32[]{:S(2)}) collective-permute-start(f32[2,40,512]{2,1,0:T(8,128)S(1)} %pad_maximum_fusion.stats), channel_id=1, source_target_pairs={{0,1},{1,0},{2,3},{3,2},{4,5},{5,4},{6,7},{7,6},{8,9},{9,8},{10,11... | collective-permute-start | bytes 491528 | tf_op jit(solution)/shard_map/ppermute | solution.py:374
  18.9 6.7 %collective-permute-start.6 = (f16[128,512]{1,0:T(8,128)(2,1)S(1)}, f16[128,512]{1,0:T(8,128)(2,1)S(1)}, u32[]{:S(2)}, u32[]{:S(2)}) collective-permute-start(f16[128,512]{1,0:T(8,128)(2,1)S(1)} %convert_element_type.82), channel_id=1, source_target_pairs={{0,2},{1,5},{2,0},{3,7},{4,6},{5,1},{6,4},{7,3},{8,10},{9,13},{10,... | collective-permute-start | bytes 393224 | tf_op jit(solution)/shard_map/ppermute | solution.py:377
  20.7 7.7 %collective-permute-start.7 = (f16[128,512]{1,0:T(8,128)(2,1)S(1)}, f16[128,512]{1,0:T(8,128)(2,1)S(1)}, u32[]{:S(2)}, u32[]{:S(2)}) collective-permute-start(f16[128,512]{1,0:T(8,128)(2,1)S(1)} %convert_element_type.81), channel_id=1, source_target_pairs={{0,4},{1,3},{2,6},{3,1},{4,0},{5,7},{6,2},{7,5},{8,12},{9,11},{10,... | collective-permute-start | bytes 393224 | tf_op jit(solution)/shard_map/ppermute | solution.py:377
  24.5 6.3 %collective-permute-start.8 = (f16[128,512]{1,0:T(8,128)(2,1)S(1)}, f16[128,512]{1,0:T(8,128)(2,1)S(1)}, u32[]{:S(2)}, u32[]{:S(2)}) collective-permute-start(f16[128,512]{1,0:T(8,128)(2,1)S(1)} %convert_element_type.83), channel_id=1, source_target_pairs={{0,2},{1,5},{2,0},{3,7},{4,6},{5,1},{6,4},{7,3},{8,10},{9,13},{10,... | collective-permute-start | bytes 393224 | tf_op jit(solution)/shard_map/ppermute | solution.py:377
  25.6 5.7 %collective-permute-start.9 = (f16[128,512]{1,0:T(8,128)(2,1)S(1)}, f16[128,512]{1,0:T(8,128)(2,1)S(1)}, u32[]{:S(2)}, u32[]{:S(2)}) collective-permute-start(f16[128,512]{1,0:T(8,128)(2,1)S(1)} %add_convert_fusion.2), channel_id=1, source_target_pairs={{0,4},{1,3},{2,6},{3,1},{4,0},{5,7},{6,2},{7,5},{8,12},{9,11},{10,... | collective-permute-start | bytes 393224 | tf_op jit(solution)/shard_map/ppermute | solution.py:377
  28.5 6.7 %collective-permute-start.11 = (f16[128,512]{1,0:T(8,128)(2,1)S(1)}, f16[128,512]{1,0:T(8,128)(2,1)S(1)}, u32[]{:S(2)}, u32[]{:S(2)}) collective-permute-start(f16[128,512]{1,0:T(8,128)(2,1)S(1)} %add_convert_fusion.1), channel_id=1, source_target_pairs={{0,2},{1,5},{2,0},{3,7},{4,6},{5,1},{6,4},{7,3},{8,10},{9,13},{10,... | collective-permute-start | bytes 393224 | tf_op jit(solution)/shard_map/ppermute | solution.py:377
  29.8 5.3 %collective-permute-start.10 = (f16[128,512]{1,0:T(8,128)(2,1)S(1)}, f16[128,512]{1,0:T(8,128)(2,1)S(1)}, u32[]{:S(2)}, u32[]{:S(2)}) collective-permute-start(f16[128,512]{1,0:T(8,128)(2,1)S(1)} %convert_element_type.86), channel_id=1, source_target_pairs={{0,4},{1,3},{2,6},{3,1},{4,0},{5,7},{6,2},{7,5},{8,12},{9,11},{10,... | collective-permute-start | bytes 393224 | tf_op jit(solution)/shard_map/ppermute | solution.py:377
  31.4 7.5 %collective-permute-start.13 = (f16[64,512]{1,0:T(8,128)(2,1)S(1)}, f16[64,512]{1,0:T(8,128)(2,1)S(1)}, u32[]{:S(2)}, u32[]{:S(2)}) collective-permute-start(f16[64,512]{1,0:T(8,128)(2,1)S(1)} %get-tuple-element.99), channel_id=1, source_target_pairs={{0,16},{8,24},{16,0},{24,8},{1,17},{9,25},{17,1},{25,9},{2,18},{10... | collective-permute-start | bytes 196616 | tf_op jit(solution)/shard_map/ppermute | solution.py:382
  33.8 6.3 %collective-permute-start.14 = (f16[64,512]{1,0:T(8,128)(2,1)S(1)}, f16[64,512]{1,0:T(8,128)(2,1)S(1)}, u32[]{:S(2)}, u32[]{:S(2)}) collective-permute-start(f16[64,512]{1,0:T(8,128)(2,1)S(1)} %get-tuple-element.100), channel_id=1, source_target_pairs={{0,24},{8,16},{16,8},{24,0},{1,25},{9,17},{17,9},{25,1},{2,26},{10... | collective-permute-start | bytes 196616 | tf_op jit(solution)/shard_map/ppermute | solution.py:382
  35.2 5.4 %collective-permute-start.12 = (f16[64,512]{1,0:T(8,128)(2,1)S(1)}, f16[64,512]{1,0:T(8,128)(2,1)S(1)}, u32[]{:S(2)}, u32[]{:S(2)}) collective-permute-start(f16[64,512]{1,0:T(8,128)(2,1)S(1)} %slice_convert_fusion), channel_id=1, source_target_pairs={{0,8},{8,0},{16,24},{24,16},{1,9},{9,1},{17,25},{25,17},{2,10},{10... | collective-permute-start | bytes 196616 | tf_op jit(solution)/shard_map/ppermute | solution.py:382
